TPU v7x, 128 devices: a whole 4x4x4 slice. The times are simulated.
128 devices in a mesh: src: 16 (over z_hi, x, core), snode: 8 (over y, z_lo).
Axes of the slice: x: 4, y: 4, z: 4 (z_hi: 2, z_lo: 2; z = z_hi * 2 + z_lo), core: 2. Of those that a mesh axis runs over, the one named last changes fastest.
Arguments:
- leaf_rhs: float32 [64, 256, 2048], P('snode', None, 'src'), may hold values from -6 to 6
- top_rhs: float32 [2048, 2048], P(None, 'src'), may hold values from -6 to 6
- leaf_inv: float32 [64, 256, 256], P('snode'), may hold values from -1 to 1, as said below
- coupling: float32 [64, 2048, 256], P('snode'), may hold values from -0.046875 to 0.046875
- top_inv: float32 [2048, 2048], P('snode'), may hold values from -1 to 1, as said below
- cond: float32 [64, 256], P('snode'), may hold values from 0.1 to 3
- electrodes: int32 [8192, 4], P('src'), may hold values from 0 to 2047, all different within a row
- blocks: int32 [16, 8192], P(None, 'src'), may hold values from 0 to 63
Outputs:
- sens: float32 [16, 256, 8192], P('snode', None, 'src')
Inputs may be any that keep to these rules, and one draw needn't show every extreme that they name: `electrodes`: the four sources of a row are different. `leaf_inv`: zero above the diagonal of each block. `top_inv`: zero above the diagonal.
All inputs are finite; a program needn't handle non-finite values.
Results may differ from a plain program's by a relative error of at most 0.00011.
Values sent between devices are 32-bit elements; how exact they have to be, the bound alone decides.
No kernel may reach another device: no remote copies, remote signals or barrier semaphores. Data moves between devices by JAX's collectives and lax.ppermute only.
A program may use at most 320 MiB of HBM per device.

v0:
```python
import jax
import jax.numpy as jnp
from jax import lax
from jax.sharding import PartitionSpec as P


def local(leaf_rhs, top_rhs, leaf_inv, coupling, top_inv, cond, electrodes, blocks):
    highest = lax.Precision.HIGHEST
    forward_leaf = jnp.einsum("bij,bjs->bis", leaf_inv, leaf_rhs, precision=highest)
    partial_value = jnp.einsum("bti,bis->ts", coupling, forward_leaf, precision=highest)
    coupled = lax.psum(partial_value, "snode")
    residual = top_rhs - coupled
    forward_top = jnp.dot(top_inv, residual, precision=highest)
    top_partial = jnp.einsum("rt,rs->ts", top_inv, forward_top, precision=highest)
    separator_field = lax.psum(top_partial, "snode")
    adjusted = forward_leaf - jnp.einsum(
        "bti,ts->bis", coupling, separator_field, precision=highest
    )
    leaf_field = jnp.einsum("bji,bjs->bis", leaf_inv, adjusted, precision=highest)
    leaves = leaf_field.shape[0]
    cells_n = leaf_field.shape[1]
    quads_n = electrodes.shape[0]
    shard_piece = lax.all_gather(leaf_field, "src", axis=2, tiled=True)
    width_n = shard_piece.shape[2]
    source_ids = lax.broadcasted_iota(jnp.int32, (width_n, quads_n), 0)

    def signed(plus_ids, minus_ids):
        upper = (source_ids == plus_ids[None, :]).astype(jnp.float32)
        lower = (source_ids == minus_ids[None, :]).astype(jnp.float32)
        return upper - lower

    current_sel = signed(electrodes[:, 0], electrodes[:, 1])
    potential_sel = signed(electrodes[:, 2], electrodes[:, 3])
    current_add = jnp.einsum("bcs,sq->bcq", shard_piece, current_sel, precision=highest)
    potential_add = jnp.einsum("bcs,sq->bcq", shard_piece, potential_sel, precision=highest)
    product = current_add * potential_add
    weighted = cond[:, :, None] * product
    owner_id = lax.axis_index("snode")
    local_blocks = blocks - owner_id * leaves
    own_rows = blocks.shape[0] // lax.axis_size("snode")
    summed = jnp.zeros((own_rows * lax.axis_size("snode"), cells_n, quads_n), jnp.float32)
    for leaf_id in range(leaves):
        summed = summed + jnp.where(
            (local_blocks == leaf_id)[:, None, :], weighted[leaf_id][None], 0.0
        )
    return lax.psum_scatter(summed, "snode", scatter_dimension=0, tiled=True)


def solution(mesh):
    return jax.shard_map(
        local,
        mesh=mesh,
        in_specs=(
            P("snode", None, "src"),
            P(None, "src"),
            P("snode", None, None),
            P("snode", None, None),
            P("snode", None),
            P("snode", None),
            P("src", None),
            P(None, "src"),
        ),
        out_specs=P("snode", None, "src"),
        check_vma=False,
    )
```

profile of v0, /device:TPU:1, one launch (start us, length us, event | category | flops | bytes accessed | tf_op | source)
XLA Modules:
  0.0 582.9 jit_solution(11139085248551137085)
XLA Ops:
  6.5 1.6 copy-done
  8.1 3.2 fusion.21
  11.3 17.3 %convolution_bitcast_fusion = f32[2048,128]{1,0:T(8,128)} fusion(f32[8,256,128]{2,1,0:T(8,128)S(1)} %fusion.21, f32[8,2048,256]{2,1,0:T(8,128)} %param.11), kind=kOutput, calls=%fused_computation.16 | convolution fusion | flops 6442450944 | bytes 18874368 | tf_op jit(solution)/shard_map/bti,bis->ts/dot_general | solution.py:10
  28.6 0.0 all-reduce.3.cloned.1.call-update
  28.6 0.0 all-reduce.5.cloned.1.call-start
  28.6 76.9 %all-reduce.3.cloned.1.call-done = f32[2048,128]{1,0:T(8,128)} async-done(((f32[2048,128]{1,0:T(8,128)}), f32[2048,128]{1,0:T(8,128)}) %all-reduce.3.cloned.1.call-update) | async-done | bytes 1048592 | tf_op jit(solution)/shard_map/psum | solution.py:11
  105.6 4.2 fusion.18
  109.8 2.2 convolution_bitcast_fusion.1
  112.0 0.0 all-reduce.5.cloned.1.call-update
  112.0 0.3 all-gather.2.cloned.1.call-start
  112.3 77.3 %all-reduce.5.cloned.1.call-done = f32[2048,128]{0,1:T(8,128)} async-done(((f32[2048,128]{0,1:T(8,128)}), f32[2048,128]{0,1:T(8,128)}) %all-reduce.5.cloned.1.call-update) | async-done | bytes 1048592 | tf_op jit(solution)/shard_map/psum | solution.py:15
  189.6 29.2 %fusion.16 = f32[8,256,128]{2,1,0:T(8,128)S(1)} fusion(f32[8,256,128]{2,1,0:T(8,128)S(1)} %fusion.21, f32[8,2048,256]{2,1,0:T(8,128)} %param.11, f32[2048,128]{0,1:T(8,128)} %all-reduce.5.cloned.1.call-done), kind=kOutput, calls=%fused_computation.24 | convolution fusion | flops 6442713088 | bytes 19922944 | tf_op jit(solution)/shard_map/bti,ts->bis/dot_general | solution.py:16
  218.8 0.0 copy-start.4
  218.9 0.0 copy-start.3
  218.9 3.0 convolution_bitcast_fusion.2
  221.9 0.0 all-gather.2.cloned.1.call-update
  221.9 0.6 reduce-scatter.2.cloned.1.call-start
  222.6 113.9 %all-gather.2.cloned.1.call-done = f32[8,256,2048]{1,2,0:T(8,128)} async-done(((f32[8,256,128]{1,2,0:T(8,128)}), f32[8,256,2048]{1,2,0:T(8,128)}) %all-gather.2.cloned.1.call-update) | async-done | bytes 16777232 | tf_op jit(solution)/shard_map/all_gather | solution.py:23
  336.5 32.1 %fusion = f32[8,256,512]{2,1,0:T(8,128)S(1)} fusion(f32[8,256,2048]{1,2,0:T(8,128)} %all-gather.2.cloned.1.call-done, s32[512]{0:T(512)S(1)} %bitcast.57, s32[512]{0:T(512)S(1)} %bitcast.58), kind=kOutput, calls=%fused_computation.1 | convolution fusion | flops 25775046656 | bytes 20975616 | tf_op jit(solution)/shard_map/bcs,sq->bcq/dot_general | solution.py:35
  368.6 30.3 %multiply_multiply_fusion = f32[8,256,512]{2,1,0:T(8,128)S(1)} fusion(f32[8,256,512]{2,1,0:T(8,128)S(1)} %fusion, f32[8,256,2048]{1,2,0:T(8,128)S(1)} %copy-done.5, s32[512]{0:T(512)S(1)} %bitcast.56, s32[512]{0:T(512)S(1)} %bitcast.55, f32[8,256]{1,0:T(8,128)S(1)} %copy-done.6), kind=kOutput, calls=%fused_computation.5 | convolution fusion | flops 25777143808 | bytes 25178112 | tf_op jit(solution)/shard_map/bcs,sq->bcq/dot_general | solution.py:34
  398.9 0.5 slice_bitcast_fusion.7
  399.3 10.2 %select_add_fusion = f32[16,256,512]{2,1,0:T(8,128)} fusion(f32[256,512]{1,0:T(8,128)S(1)} %get-tuple-element.6, f32[256,512]{1,0:T(8,128)S(1)} %get-tuple-element.7, f32[256,512]{1,0:T(8,128)S(1)} %get-tuple-element.8, f32[256,512]{1,0:T(8,128)S(1)} %get-tuple-element.9, f32[256,512]{1,0:T(8,128)S(1)} %get-tuple-element.10, ...), kind=kLoop, calls=%fused_computation | loop fusion | flops 31457280 | bytes 12648448 | tf_op jit(solution)/shard_map/add | solution.py:43
  409.5 0.0 reduce-scatter.2.cloned.1.call-update
  409.5 166.6 %reduce-scatter.2.cloned.1.call-done = f32[2,256,512]{2,1,0:T(8,128)} async-done(((f32[16,256,512]{2,1,0:T(8,128)}), f32[2,256,512]{2,1,0:T(8,128)}) %reduce-scatter.2.cloned.1.call-update) | async-done | bytes 1048592 | tf_op jit(solution)/shard_map/reduce_scatter | solution.py:46
  (14 shorter events, 0.1 us)
Async XLA Ops:
  6.5 1.6 copy-start
  6.5 99.0 %all-reduce.3.cloned.1.call-start = ((), (), s32[]{:S(2)}) async-start(), calls=%async_computation.1 | async-start | bytes 2097152 | tf_op jit(solution)/shard_map/psum | solution.py:11
  28.6 161.1 %all-reduce.5.cloned.1.call-start = ((), (), s32[]{:S(2)}) async-start(), calls=%async_computation.2 | async-start | bytes 2097152 | tf_op jit(solution)/shard_map/psum | solution.py:15
  105.5 4.2 copy-start.2
  112.0 224.5 %all-gather.2.cloned.1.call-start = ((), (), s32[]{:S(2)}) async-start(), calls=%async_computation.3 | async-start | bytes 17825792 | tf_op jit(solution)/shard_map/all_gather | solution.py:23
  218.8 3.6 copy-start.4
  218.9 3.6 copy-start.3
  221.9 354.2 %reduce-scatter.2.cloned.1.call-start = ((), (), s32[]{:S(2)}) async-start(), calls=%async_computation.4 | async-start | bytes 9437184 | tf_op jit(solution)/shard_map/reduce_scatter | solution.py:46
  336.5 32.1 %copy-start.5 = (f32[8,256,2048]{1,2,0:T(8,128)S(1)}, f32[8,256,2048]{1,2,0:T(8,128)}, u32[]{:S(2)}) copy-start(f32[8,256,2048]{1,2,0:T(8,128)} %all-gather.2.cloned.1.call-done) | copy-start | bytes 50331652
  336.5 32.1 %copy-start.6 = (f32[8,256]{1,0:T(8,128)S(1)}, f32[8,256]{1,0:T(8,128)}, u32[]{:S(2)}) copy-start(f32[8,256]{1,0:T(8,128)} %param.13) | copy-start | bytes 24580
  409.5 166.6 %copy-start.1 = (f32[8,256,256]{2,1,0:T(8,128)S(1)}, f32[8,256,256]{2,1,0:T(8,128)}, u32[]{:S(2)}) copy-start(f32[8,256,256]{2,1,0:T(8,128)} %param.10) | copy-start | bytes 6291460
Sparse Core Ops, SparseCore 0:
  28.7 76.7 all-reduce.2
  112.1 77.4 all-reduce.4
  222.0 114.4 all-gather.1
  409.7 166.3 reduce-scatter.1
where the time goes:
time: 590 us; the launch traced here: 583 us
  waiting for transfers between devices  435 us (74%)
  matrix products  121 us (21%)
  between operations  13.5 us (2%)
  other arithmetic  10.2 us (2%)
    reduce_scatter x1, waiting for transfers between devices, local(): return lax.psum_scatter(summed, 'snode', scatter_dimension=0, tiled=True)  167 us
    all_gather x1, waiting for transfers between devices, local(): shard_piece = lax.all_gather(leaf_field, 'src', axis=2, tiled=True)  114 us
    psum x1, waiting for transfers between devices, local(): separator_field = lax.psum(top_partial, 'snode')  77.3 us
    psum x1, waiting for transfers between devices, local(): coupled = lax.psum(partial_value, 'snode')  76.9 us
    dot_general x1, matrix products, local(): jnp.einsum('bcs,sq->bcq', shard_piece, potential_sel, precision=highest)  32.1 us
    dot_general x1, matrix products, local(): jnp.einsum('bcs,sq->bcq', shard_piece, current_sel, precision=highest)  30.3 us
    dot_general x1, matrix products, local(): jnp.einsum('bti,ts->bis', coupling, separator_field, precision=highest)  29.2 us
    dot_general x1, matrix products, local(): jnp.einsum('bti,bis->ts', coupling, forward_leaf, precision=highest)  17.3 us
  transfers between devices with their start and end apart: 4, of which 4 were waited for; matrix products, arithmetic and copies ran while one was open for 0% of the time, Pallas kernels for 0%

commit v1 on v0

--- a/solution.py
+++ b/solution.py
@@ -1,7 +1,17 @@
+import functools
 import jax
 import jax.numpy as jnp
 from jax import lax
 from jax.sharding import PartitionSpec as P
+
+
+def _produce_target(xx, row_dim):
+    back = jnp.stack([xx] * lax.axis_size("src"))
+    latest = lax.all_to_all(back, split_axis=0, concat_axis=0, axis_name="src")
+    return jnp.concatenate(latest, axis=row_dim)
+
+
+assign_the_tokens = functools.partial(_produce_target, row_dim=2)
 
 
 def local(leaf_rhs, top_rhs, leaf_inv, coupling, top_inv, cond, electrodes, blocks):
@@ -20,7 +30,7 @@
     leaves = leaf_field.shape[0]
     cells_n = leaf_field.shape[1]
     quads_n = electrodes.shape[0]
-    shard_piece = lax.all_gather(leaf_field, "src", axis=2, tiled=True)
+    shard_piece = assign_the_tokens(leaf_field)
     width_n = shard_piece.shape[2]
     source_ids = lax.broadcasted_iota(jnp.int32, (width_n, quads_n), 0)
 

time: 590 us -> 723 us (1.23)
  waiting for transfers between devices: 435 us -> 548 us
  starting transfers between devices: 0.94 us -> 11.5 us
  local copies, waits for them, and re-layouts: 2.08 us -> 10.3 us
    all_to_all x0 -> x1, waiting for transfers between devices: none -> 224 us  [_produce_target(): latest = lax.all_to_all(back, split_axis=0, concat_axis=0, axis_name='src')]
    all_gather x1 -> x0, waiting for transfers between devices: 114 us -> none  [local(): shard_piece = lax.all_gather(leaf_field, 'src', axis=2, tiled=True)]
    all_to_all x0 -> x1, starting transfers between devices: none -> 11.4 us  [_produce_target(): latest = lax.all_to_all(back, split_axis=0, concat_axis=0, axis_name='src')]
    another operation x0 -> x1, local copies, waits for them, and re-layouts: none -> 7.91 us  [_produce_target(): back = jnp.stack([xx] * lax.axis_size('src'))]
where the time goes in v1:
time: 723 us; the launch traced here: 716 us
  waiting for transfers between devices  548 us (76%)
  matrix products  123 us (17%)
  between operations  13.5 us (2%)
  starting transfers between devices  11.5 us (2%)
  local copies, waits for them, and re-layouts  10.3 us (1%)
  other arithmetic  10 us (1%)
    all_to_all x1, waiting for transfers between devices, _produce_target(): latest = lax.all_to_all(back, split_axis=0, concat_axis=0, axis_name='src')  224 us
    reduce_scatter x1, waiting for transfers between devices, local(): return lax.psum_scatter(summed, 'snode', scatter_dimension=0, tiled=True)  169 us
    psum x1, waiting for transfers between devices, local(): separator_field = lax.psum(top_partial, 'snode')  77.6 us
    psum x1, waiting for transfers between devices, local(): coupled = lax.psum(partial_value, 'snode')  76.9 us
    dot_general x1, matrix products, local(): jnp.einsum('bcs,sq->bcq', shard_piece, current_sel, precision=highest)  32.5 us
    dot_general x1, matrix products, local(): jnp.einsum('bcs,sq->bcq', shard_piece, potential_sel, precision=highest)  32.4 us
    dot_general x1, matrix products, local(): jnp.einsum('bti,ts->bis', coupling, separator_field, precision=highest)  29.6 us
    dot_general x1, matrix products, local(): jnp.einsum('bti,bis->ts', coupling, forward_leaf, precision=highest)  17.3 us
  transfers between devices with their start and end apart: 4, of which 4 were waited for; matrix products, arithmetic and copies ran while one was open for 0% of the time, Pallas kernels for 0%

profile of v1, /device:TPU:1, one launch (start us, length us, event | category | flops | bytes accessed | tf_op | source)
XLA Modules:
  0.0 716.2 jit_solution(14421967778257465576)
XLA Ops:
  6.5 0.0 all-reduce.3.cloned.1.call-start
  6.5 1.6 copy-done
  8.1 3.2 fusion.27
  11.3 17.3 %convolution_bitcast_fusion = f32[2048,128]{1,0:T(8,128)} fusion(f32[8,256,128]{2,1,0:T(8,128)S(1)} %fusion.27, f32[8,2048,256]{2,1,0:T(8,128)} %param.11), kind=kOutput, calls=%fused_computation.20 | convolution fusion | flops 6442450944 | bytes 18874368 | tf_op jit(solution)/shard_map/bti,bis->ts/dot_general | solution.py:20
  28.6 0.0 all-reduce.3.cloned.1.call-update
  28.6 0.0 all-reduce.5.cloned.1.call-start
  28.6 76.9 %all-reduce.3.cloned.1.call-done = f32[2048,128]{1,0:T(8,128)} async-done(((f32[2048,128]{1,0:T(8,128)}), f32[2048,128]{1,0:T(8,128)}) %all-reduce.3.cloned.1.call-update) | async-done | bytes 1048592 | tf_op jit(solution)/shard_map/psum | solution.py:21
  105.6 4.2 fusion.24
  109.8 2.2 convolution_bitcast_fusion.1
  112.0 0.0 all-reduce.5.cloned.1.call-update
  112.0 77.6 %all-reduce.5.cloned.1.call-done = f32[2048,128]{0,1:T(8,128)} async-done(((f32[2048,128]{0,1:T(8,128)}), f32[2048,128]{0,1:T(8,128)}) %all-reduce.5.cloned.1.call-update) | async-done | bytes 1048592 | tf_op jit(solution)/shard_map/psum | solution.py:25
  189.6 29.6 %fusion.22 = f32[8,256,128]{2,1,0:T(8,128)S(1)} fusion(f32[8,256,128]{2,1,0:T(8,128)S(1)} %fusion.27, f32[8,2048,256]{2,1,0:T(8,128)} %param.11, f32[2048,128]{0,1:T(8,128)} %all-reduce.5.cloned.1.call-done), kind=kOutput, calls=%fused_computation.28 | convolution fusion | flops 6442713088 | bytes 19922944 | tf_op jit(solution)/shard_map/bti,ts->bis/dot_general | solution.py:26
  219.3 2.0 convolution_bitcast_fusion.2
  221.3 0.3 copy.12
  221.7 7.9 %stack.2 = f32[16,8,256,128]{3,2,1,0:T(8,128)} broadcast(f32[8,256,128]{2,1,0:T(8,128)S(1)} %copy.12), dimensions={1,2,3} | broadcast | bytes 17825792 | tf_op jit(solution)/shard_map/stack | solution.py:9
  229.6 11.4 %all-to-all-start = ((f32[16,8,256,128]{3,2,1,0:T(8,128)}), f32[16,8,256,128]{3,2,1,0:T(8,128)}, u32[]{:S(2)}, u32[]{:S(2)}) async-start(f32[16,8,256,128]{3,2,1,0:T(8,128)} %stack.2), calls=%async_computation | async-start | bytes 33554432 | tf_op jit(solution)/shard_map/all_to_all | solution.py:10
  241.0 0.0 reduce-scatter.2.cloned.1.call-start
  241.2 224.3 %all-to-all-done = f32[16,8,256,128]{3,2,1,0:T(8,128)} async-done(((f32[16,8,256,128]{3,2,1,0:T(8,128)}), f32[16,8,256,128]{3,2,1,0:T(8,128)}, u32[]{:S(2)}, u32[]{:S(2)}) %all-to-all-start) | async-done | bytes 16777248 | tf_op jit(solution)/shard_map/all_to_all | solution.py:10
  465.5 32.4 %fusion = f32[8,256,512]{2,1,0:T(8,128)S(1)} fusion(s32[512]{0:T(512)S(1)} %bitcast.70, s32[512]{0:T(512)S(1)} %bitcast.71, f32[16,8,256,128]{3,2,1,0:T(8,128)} %all-to-all-done), kind=kOutput, calls=%fused_computation | convolution fusion | flops 25775046656 | bytes 20975616 | tf_op jit(solution)/shard_map/bcs,sq->bcq/dot_general | solution.py:45
  497.9 32.5 %multiply_multiply_fusion = f32[8,256,512]{2,1,0:T(8,128)S(1)} fusion(f32[8,256,512]{2,1,0:T(8,128)S(1)} %fusion, s32[512]{0:T(512)S(1)} %bitcast.69, s32[512]{0:T(512)S(1)} %bitcast.68, f32[8,256]{1,0:T(8,128)S(1)} %copy-done.5, f32[16,8,256,128]{3,2,1,0:T(8,128)} %all-to-all-done), kind=kOutput, calls=%fused_computation.9 | convolution fusion | flops 25777143808 | bytes 25178112 | tf_op jit(solution)/shard_map/bcs,sq->bcq/dot_general | solution.py:44
  530.4 0.5 slice_bitcast_fusion.7
  530.8 10.0 %select_add_fusion = f32[16,256,512]{2,1,0:T(8,128)} fusion(f32[256,512]{1,0:T(8,128)S(1)} %get-tuple-element.6, f32[256,512]{1,0:T(8,128)S(1)} %get-tuple-element.7, f32[256,512]{1,0:T(8,128)S(1)} %get-tuple-element.8, f32[256,512]{1,0:T(8,128)S(1)} %get-tuple-element.9, f32[256,512]{1,0:T(8,128)S(1)} %get-tuple-element.10, ...), kind=kLoop, calls=%fused_computation.6 | loop fusion | flops 31457280 | bytes 12648448 | tf_op jit(solution)/shard_map/add | solution.py:53
  540.8 0.0 reduce-scatter.2.cloned.1.call-update
  540.8 168.6 %reduce-scatter.2.cloned.1.call-done = f32[2,256,512]{2,1,0:T(8,128)} async-done(((f32[16,256,512]{2,1,0:T(8,128)}), f32[2,256,512]{2,1,0:T(8,128)}) %reduce-scatter.2.cloned.1.call-update) | async-done | bytes 1048592 | tf_op jit(solution)/shard_map/reduce_scatter | solution.py:56
  (13 shorter events, 0.1 us)
Async XLA Ops:
  6.5 1.6 copy-start
  6.5 99.0 %all-reduce.3.cloned.1.call-start = ((), (), s32[]{:S(2)}) async-start(), calls=%async_computation.2 | async-start | bytes 2097152 | tf_op jit(solution)/shard_map/psum | solution.py:21
  28.6 161.1 %all-reduce.5.cloned.1.call-start = ((), (), s32[]{:S(2)}) async-start(), calls=%async_computation.3 | async-start | bytes 2097152 | tf_op jit(solution)/shard_map/psum | solution.py:25
  105.5 4.2 copy-start.2
  229.6 11.5 %copy-start.4 = (s32[512,4]{0,1:T(4,128)S(1)}, s32[512,4]{0,1:T(4,128)}, u32[]{:S(2)}) copy-start(s32[512,4]{0,1:T(4,128)} %param.14) | copy-start | bytes 24580
  229.6 11.5 %copy-start.3 = (s32[16,512]{1,0:T(8,128)S(1)}, s32[16,512]{1,0:T(8,128)}, u32[]{:S(2)}) copy-start(s32[16,512]{1,0:T(8,128)} %param.15) | copy-start | bytes 98308
  229.6 235.9 %all-to-all-start = ((f32[16,8,256,128]{3,2,1,0:T(8,128)}), f32[16,8,256,128]{3,2,1,0:T(8,128)}, u32[]{:S(2)}, u32[]{:S(2)}) async-start(f32[16,8,256,128]{3,2,1,0:T(8,128)} %stack.2), calls=%async_computation | async-start | bytes 33554432 | tf_op jit(solution)/shard_map/all_to_all | solution.py:10
  241.0 468.4 %reduce-scatter.2.cloned.1.call-start = ((), (), s32[]{:S(2)}) async-start(), calls=%async_computation.4 | async-start | bytes 9437184 | tf_op jit(solution)/shard_map/reduce_scatter | solution.py:56
  465.5 32.4 %copy-start.5 = (f32[8,256]{1,0:T(8,128)S(1)}, f32[8,256]{1,0:T(8,128)}, u32[]{:S(2)}) copy-start(f32[8,256]{1,0:T(8,128)} %param.13) | copy-start | bytes 24580
  540.8 168.6 %copy-start.1 = (f32[8,256,256]{2,1,0:T(8,128)S(1)}, f32[8,256,256]{2,1,0:T(8,128)}, u32[]{:S(2)}) copy-start(f32[8,256,256]{2,1,0:T(8,128)} %param.10) | copy-start | bytes 6291460
Sparse Core Ops, SparseCore 0:
  28.7 76.7 all-reduce.2
  112.1 77.4 all-reduce.4
  541.0 168.4 reduce-scatter.1
